TPU v7x, 768 devices: a whole 4x8x12 slice. The times are simulated.
768 devices in a mesh: dp: 64 (over x, y, core), mp: 12 (over z).
Axes of the slice: x: 4, y: 8, z: 12, core: 2. Of those that a mesh axis runs over, the one named last changes fastest.
Arguments:
- features: bfloat16 [30720, 24576], P('dp', 'mp'), may hold values from -6 to 6
- segment: int32 [30720], P(('dp', 'mp')), may hold values from 0 to 1919, never falling along the last dimension, each value on 1 to 48 neighbouring positions
- gains: float32 [3, 8192], replicated, may hold values from 0.25 to 1.75
Outputs:
- mixed: bfloat16 [30720, 8192], P(('dp', 'mp'))
- grad_gains: float32 [3, 8192], replicated
- row_loss: float32 [30720], P(('dp', 'mp'))
Inputs may be any that keep to these rules, and one draw needn't show every extreme that they name: `segment`: never falls along the rows; each response spans 1 to 48 rows and one spans exactly 48.
All inputs are finite; a program needn't handle non-finite values.
Results may differ from a plain program's by a relative error of at most 0.001.
Values may be sent and summed in bfloat16 or wider, within the bound.
A program may use at most 64 MiB of HBM per device.

v0:
```python
import jax
import jax.numpy as jnp
from jax import lax
from jax.sharding import PartitionSpec as P


def passed_along(shard, axis, by):
    peers = lax.axis_size(axis)
    pairs = [(i, i + by) for i in range(peers) if 0 <= i + by < peers]
    return lax.ppermute(shard, axis, pairs)


def shards(features, segment, gains):
    rows = lax.all_to_all(features, "mp", split_axis=0, concat_axis=1, tiled=True)
    count = rows.shape[0]
    width = gains.shape[1]
    x = rows.astype(jnp.float32).reshape(count, 3, width)
    scale = 1.0 / jnp.sqrt(jnp.mean(x * x, axis=2, keepdims=True) + 1e-06)
    unit = x * scale
    joined = jnp.sum(unit * gains[None], axis=1) / 3.0
    first_high = rows[:1, 2 * width :]
    first_seg = segment[:1] + 1
    recv_high, recv_seg = passed_along((first_high, first_seg), ("dp", "mp"), -1)
    high = jnp.concatenate([rows[1:, 2 * width :], recv_high], axis=0).astype(jnp.float32)
    target = high / jnp.sqrt(jnp.mean(high * high, axis=1, keepdims=True) + 1e-06)
    next_seg = jnp.concatenate([segment[1:], recv_seg - 1], axis=0)
    valid = (next_seg == segment).astype(jnp.float32)
    error = joined - target
    size = jnp.abs(error)
    huber = jnp.where(size <= 1.0, 0.5 * error * error, size - 0.5)
    row_loss = valid * jnp.mean(huber, axis=1)
    slope = valid[:, None] * jnp.clip(error, -1.0, 1.0)
    total_rows = count * lax.axis_size("dp") * lax.axis_size("mp")
    local_grad = jnp.sum(slope[:, None, :] * unit, axis=0) / (
        3.0 * jnp.sqrt(jnp.float32(total_rows))
    )
    grad_gains = lax.psum(local_grad, ("dp", "mp"))
    return (joined.astype(jnp.bfloat16), grad_gains, row_loss)


def solution(mesh):
    return jax.shard_map(
        shards,
        mesh=mesh,
        in_specs=(P("dp", "mp"), P(("dp", "mp")), P()),
        out_specs=(P(("dp", "mp"), None), P(), P(("dp", "mp"))),
        check_vma=False,
    )
```

profile of v0, /device:TPU:1, one launch (start us, length us, event | category | flops | bytes accessed | tf_op | source)
XLA Modules:
  0.0 601.4 jit_solution(14028063946756049229)
XLA Ops:
  7.2 15.7 %all-to-all-start = ((bf16[12,40,2048]{2,1,0:T(8,128)(2,1)}), bf16[12,40,2048]{2,1,0:T(8,128)(2,1)S(1)}, u32[]{:S(2)}, u32[]{:S(2)}) async-start(bf16[12,40,2048]{2,1,0:T(8,128)(2,1)} %bitcast.17), calls=%async_computation | async-start | bytes 3932160 | tf_op jit(solution)/shard_map/all_to_all | solution.py:14
  23.0 52.3 %collective-permute-start = (s32[1]{0:T(128)}, s32[1]{0:T(128)}, u32[]{:S(2)}, u32[]{:S(2)}) collective-permute-start(s32[1]{0:T(128)} %add.31), channel_id=1, source_target_pairs={{1,0},{2,1},{3,2},{4,3},{5,4},{6,5},{7,6},{8,7},{9,8},{10,9},{11,1... | collective-permute-start | bytes 20 | tf_op jit(solution)/shard_map/ppermute | solution.py:10
  75.4 9.2 %collective-permute-done = s32[1]{0:T(128)} collective-permute-done((s32[1]{0:T(128)}, s32[1]{0:T(128)}, u32[]{:S(2)}, u32[]{:S(2)}) %collective-permute-start) | collective-permute-done | bytes 36 | tf_op jit(solution)/shard_map/ppermute | solution.py:10
  85.3 5.0 all-to-all-done
  90.3 0.1 copy.17
  90.5 1.2 copy-done
  91.7 5.9 collective-permute-start.1
  97.6 0.5 bitcast_convert_fusion
  98.1 4.7 copy.13
  102.8 8.0 %reshape.81 = f32[40,3,8192]{2,1,0:T(4,128)} reshape(f32[40,12,2048]{2,1,0:T(8,128)} %copy.13) | data formatting | bytes 7864320 | tf_op jit(solution)/shard_map/convert_element_type | solution.py:17
  110.8 0.5 multiply_reduce_fusion.1
  111.4 0.3 copy-done.1
  111.7 7.4 %multiply_reduce_fusion = f32[40,8192]{1,0:T(8,128)} fusion(f32[40,3,8192]{2,1,0:T(4,128)} %reshape.81, f32[3,8192]{1,0:T(4,128)S(1)} %copy-done.1, f32[40,3]{1,0:T(8,128)S(1)} %copy.14), kind=kLoop, calls=%fused_computation | loop fusion | flops 2621440 | bytes 5341664 | tf_op jit(solution)/shard_map/reduce_sum | solution.py:20
  119.1 1.2 slice.16
  120.4 0.3 fusion.1
  120.7 2.9 fusion.4
  123.5 0.6 multiply_select_fusion
  124.1 0.2 clamp_multiply_fusion
  124.3 3.8 mul.72
  128.1 8.0 %mul.73 = f32[40,12,2048]{2,1,0:T(8,128)} reshape(f32[40,3,8192]{2,1,0:T(4,128)} %mul.72) | data formatting | bytes 7864320 | tf_op jit(solution)/shard_map/mul | solution.py:34
  136.0 5.1 fusion
  141.1 0.7 div.54
  141.9 451.1 %all-reduce.2.cloned.1.call-done = f32[3,8192]{1,0:T(4,128)} async-done(((f32[3,8192]{1,0:T(4,128)}), f32[3,8192]{1,0:T(4,128)}) %all-reduce.2.cloned.1.call-update) | async-done | bytes 98320 | tf_op jit(solution)/shard_map/psum | solution.py:37
  593.0 1.6 copy.22
  (18 shorter events, 0.3 us)
Async XLA Ops:
  7.2 15.8 %copy-start.2 = (s32[40]{0:T(128)S(1)}, s32[40]{0:T(128)}, u32[]{:S(2)}) copy-start(s32[40]{0:T(128)} %param.4) | copy-start | bytes 484
  7.2 83.1 %all-to-all-start = ((bf16[12,40,2048]{2,1,0:T(8,128)(2,1)}), bf16[12,40,2048]{2,1,0:T(8,128)(2,1)S(1)}, u32[]{:S(2)}, u32[]{:S(2)}) async-start(bf16[12,40,2048]{2,1,0:T(8,128)(2,1)} %bitcast.17), calls=%async_computation | async-start | bytes 3932160 | tf_op jit(solution)/shard_map/all_to_all | solution.py:14
  22.9 570.1 %all-reduce.2.cloned.1.call-start = ((), (), s32[]{:S(2)}) async-start(), calls=%async_computation.1 | async-start | bytes 262144 | tf_op jit(solution)/shard_map/psum | solution.py:37
  23.0 61.7 %collective-permute-start = (s32[1]{0:T(128)}, s32[1]{0:T(128)}, u32[]{:S(2)}, u32[]{:S(2)}) collective-permute-start(s32[1]{0:T(128)} %add.31), channel_id=1, source_target_pairs={{1,0},{2,1},{3,2},{4,3},{5,4},{6,5},{7,6},{8,7},{9,8},{10,9},{11,1... | collective-permute-start | bytes 20 | tf_op jit(solution)/shard_map/ppermute | solution.py:10
  90.4 1.3 copy-start
  91.7 28.7 %collective-permute-start.1 = (bf16[1,8192]{1,0:T(2,128)(2,1)S(1)}, bf16[1,8192]{1,0:T(2,128)(2,1)S(1)}, u32[]{:S(2)}, u32[]{:S(2)}) collective-permute-start(bf16[1,8192]{1,0:T(2,128)(2,1)S(1)} %slice.17), channel_id=1, source_target_pairs={{1,0},{2,1},{3,2},{4,3},{5,4},{6,5},{7,6},{8,7},{9,8},{10,9},{11,1... | collective-permute-start | bytes 49160 | tf_op jit(solution)/shard_map/ppermute | solution.py:10
  110.8 0.9 copy-start.1
Sparse Core Ops, SparseCore 0:
  142.0 450.9 all-reduce.1
where the time goes:
time: 603 us; the launch traced here: 601 us
  waiting for transfers between devices  465 us (77%)
  starting transfers between devices  74 us (12%)
  local copies, waits for them, and re-layouts  29.9 us (5%)
  other arithmetic  17.3 us (3%)
  between operations  14.9 us (2%)
    psum x1, waiting for transfers between devices, shards(): grad_gains = lax.psum(local_grad, ('dp', 'mp'))  451 us
    ppermute x2, starting transfers between devices, passed_along(): return lax.ppermute(shard, axis, pairs)  58.3 us
    all_to_all x1, starting transfers between devices, shards(): lax.all_to_all(features, 'mp', split_axis=0, concat_axis=1, tiled=True)  15.7 us
    convert_element_type x2, local copies, waits for them, and re-layouts, shards(): x = rows.astype(jnp.float32).reshape(count, 3, width)  12.7 us
  transfers between devices with their start and end apart: 4, of which 3 were waited for; matrix products, arithmetic and copies ran while one was open for 4% of the time, Pallas kernels for 0%

commit v1 on v0

v1 whole, which is shorter than its diff:
```python
import functools
import math

import jax
import jax.numpy as jnp
from jax import lax
from jax.experimental import pallas as pl
from jax.experimental.pallas import tpu as pltpu
from jax.sharding import PartitionSpec as P

LEVELS = 3
QUARTERS = 4
RING = LEVELS * QUARTERS
HALVES = 6
CHUNK = 16
EPS = 1e-06
F32 = jnp.float32
BF16 = jnp.bfloat16


def first_half(level, quarter):
    return (2 * level + (quarter + 1) // 2 - 1 + HALVES) % HALVES


def handler_level(half, quarter):
    return (((half + HALVES + 1 - (quarter + 1) // 2) % HALVES)) // 2


def kernel(sizes, feat, seg, gains, mixed, grads, row_loss, fbuf, xbuf, gbuf, mixbuf, obuf, m1, nr, nrs, nrstage, nrn, nxt,
           sq, segs, scp, cols, val, acc, lq, lrow, lbuf, part, ra, sa, rb, sb, rc, gd,
           local_sem, p1_send, p1_recv, m1_send, m1_recv, mx_send, mx_recv, nr_send, nr_recv, p2_send, p2_recv,
           ls_send, ls_recv, ar_send, ar_recv):
    groups, nx, ny, nk, own, width, total_rows = sizes
    half = 2 * own
    group_rows = HALVES * half
    per_half = half // CHUNK
    chunks = 2 * per_half
    blocks = width // 128
    per_piece = blocks // ny
    lanes = m1.shape[2] - 128

    g, z = lax.axis_index("dp"), lax.axis_index("mp")
    level, quarter = z // QUARTERS, z % QUARTERS
    a = first_half(level, quarter)
    kc = g % nk
    y = (g // nk) % ny
    x = g // (nk * ny)

    def remote(src, dst, send, recv, gd_, zd_):
        return pltpu.make_async_remote_copy(
            src_ref=src, dst_ref=dst, send_sem=send, recv_sem=recv,
            device_id=(gd_, zd_), device_id_type=pl.DeviceIdType.MESH)

    def y_peer(j):
        return (x * ny + (y + j) % ny) * nk + kc

    def xk_peer(j):
        n = (x * nk + kc + j) % (nx * nk)
        return ((n // nk) * ny + y) * nk + n % nk

    loads = []
    for h in range(HALVES):
        loads.append(pltpu.make_async_copy(
            feat.at[pl.ds(h * half, half), :], fbuf.at[pl.ds(h * half, half), :], local_sem.at[h]))
        loads[-1].start()
    gain_load = pltpu.make_async_copy(
        gains.at[:, pl.ds(pl.multiple_of(quarter * width, width), width)], gbuf, local_sem.at[HALVES])
    gain_load.start()
    own_loads = []
    for s in range(2):
        row = pl.multiple_of(((a + s) % HALVES) * half, half)
        own_loads.append(pltpu.make_async_copy(
            feat.at[pl.ds(row, half), :], xbuf.at[level, pl.ds(s * half, half), :], local_sem.at[HALVES + 1 + s]))
        own_loads[-1].start()

    m1[pl.ds(RING, 5), :, 0:lanes] = jnp.zeros((5, 1, lanes), F32)
    m1[pl.ds(RING, 5), :, lanes:lanes + 128] = jnp.full((5, 1, 128), -1.0, F32)
    nr[...] = jnp.zeros(nr.shape, BF16)

    sends_back = jnp.logical_and(jnp.logical_or(z == 0, z >= 2 * QUARTERS), g > 0)
    hears_next = jnp.logical_and(jnp.logical_or(z == 0, z > 2 * QUARTERS), g < groups - 1)
    edge_in = (0, 9, 10, 11)
    edge_out = (8, 9, 10, 11, 0)
    barrier = pltpu.get_barrier_semaphore()

    def greet(gd_, zd_):
        pl.semaphore_signal(barrier, inc=1, device_id=(gd_, zd_), device_id_type=pl.DeviceIdType.MESH)

    for j in range(1, RING):
        greet(g, (z + j) % RING)
    for j in range(1, ny):
        greet(y_peer(j), z)
    for j in range(1, nx * nk):
        greet(xk_peer(j), z)

    @pl.when(sends_back)
    def _():
        for zd in edge_in:
            greet(g - 1, zd)

    @pl.when(hears_next)
    def _():
        for zd in edge_out:
            greet(g + 1, zd)

    sq[pl.ds(group_rows, sq.shape[0] - group_rows), :] = jnp.zeros((sq.shape[0] - group_rows, 128), F32)
    for h in range(HALVES):
        loads[h].wait()

        def squares(i, _):
            row = pl.multiple_of(h * half + i * CHUNK, CHUNK)
            total = jnp.zeros((CHUNK, 128), F32)
            for b in range(blocks):
                v = fbuf[pl.ds(row, CHUNK), 128 * b:128 * b + 128].astype(F32)
                total = total + v * v
            sq[pl.ds(row, CHUNK), :] = total
            return 0

        lax.fori_loop(0, per_half, squares, 0)
    m1[z, :, 0:lanes] = jnp.sum(sq[...].T, axis=0, keepdims=True)
    m1[z, :, lanes:lanes + 128] = seg[...]

    @pl.when(level == LEVELS - 1)
    def _():
        nrs[...] = jnp.zeros(nrs.shape, F32)
        for h in range(HALVES):
            row = ((h + 1) * half) % group_rows
            for b in range(blocks):
                nrs[b:b + 1, :] = fbuf[row:row + CHUNK, 128 * b:128 * b + 128].astype(F32)[0:1, :]
            nrstage[h] = nrs[...].astype(BF16)

    pl.semaphore_wait(
        barrier,
        (RING - 1) + (ny - 1) + (nx * nk - 1) + jnp.where(sends_back, 4, 0) + jnp.where(hears_next, 5, 0))

    def m1_copy(j):
        return remote(m1.at[z], m1.at[z], m1_send.at[j - 1], m1_recv.at[j - 1], g, (z + j) % RING)

    for j in range(1, RING):
        m1_copy(j).start()

    edge_slot = jnp.where(z == 0, 4, quarter)

    def edge_copy(i):
        return remote(m1.at[z], m1.at[RING + edge_slot], mx_send.at[i], mx_recv.at[edge_slot], g - 1, edge_in[i])

    @pl.when(sends_back)
    def _():
        for i in range(4):
            edge_copy(i).start()

    def next_copy(h):
        to = handler_level(h, quarter)
        slot = (h - first_half(to, quarter) + HALVES) % HALVES
        gd_ = g - 1 if h == HALVES - 1 else g
        return remote(nrstage.at[h], nr.at[slot], nr_send.at[h], nr_recv.at[slot], gd_, QUARTERS * to + quarter)

    def next_goes(h):
        if h == HALVES - 1:
            return jnp.logical_and(level == LEVELS - 1, g > 0)
        return jnp.logical_and(level == LEVELS - 1, handler_level(h, quarter) != LEVELS - 1)

    for h in range(HALVES):
        @pl.when(next_goes(h))
        def _():
            next_copy(h).start()

        if h != HALVES - 1:
            @pl.when(jnp.logical_and(level == LEVELS - 1, handler_level(h, quarter) == LEVELS - 1))
            def _():
                slot = (h - first_half(LEVELS - 1, quarter) + HALVES) % HALVES
                nr[slot] = nrstage[h]

    def level_copy(d, k):
        to = (level + d) % LEVELS
        s, kk = k // per_half, k % per_half
        row = ((first_half(to, quarter) + s) % HALVES) * half + kk * CHUNK
        return remote(
            feat.at[pl.ds(pl.multiple_of(row, CHUNK), CHUNK), :],
            xbuf.at[level, pl.ds(pl.multiple_of(k * CHUNK, CHUNK), CHUNK), :],
            p1_send.at[d - 1, k], p1_recv.at[d - 1, k], g, QUARTERS * to + quarter)

    def level_start(i, _):
        k = chunks - 1 - i
        level_copy(1, k).start()
        level_copy(2, k).start()
        return 0

    lax.fori_loop(0, chunks, level_start, 0)

    acc[...] = jnp.zeros(acc.shape, F32)
    lq[...] = jnp.zeros(lq.shape, F32)
    scp[...] = jnp.zeros(scp.shape, F32)
    segs[...] = jnp.zeros(segs.shape, F32)
    gain_load.wait()
    gbuf[...] = gbuf[...] * (1.0 / LEVELS)

    for j in range(1, RING):
        m1_copy(j).wait_recv()

    @pl.when(hears_next)
    def _():
        for i in range(5):
            remote(m1.at[z], m1.at[RING + i], mx_send.at[0], mx_recv.at[i], g, (z + 1) % RING).wait_recv()

    def scale_of(first):
        total = m1[first, :, 0:lanes]
        for i in range(1, QUARTERS):
            total = total + m1[first + i, :, 0:lanes]
        return 1.0 / jnp.sqrt(total * (1.0 / (QUARTERS * width)) + EPS)

    for l in range(LEVELS):
        scp[l:l + 1, :] = scale_of(QUARTERS * l)
    for o in range(RING):
        segs[o:o + 1, :] = m1[o, :, lanes:lanes + 128]
    segs[RING:RING + 1, :] = m1[RING + 4, :, lanes:lanes + 128]
    here = segs[...]
    lane = lax.broadcasted_iota(jnp.int32, here.shape, 1)
    after = jnp.where(lane == own - 1, pltpu.roll(pltpu.roll(here, 15, 0), own - 1, 1), pltpu.roll(here, 127, 1))
    scp[16:32, 0:128] = jnp.where(after == here, 1.0, 0.0)
    cols[...] = scp[...].T
    for o in range(RING):
        val[own * o:own * o + own, :] = jnp.broadcast_to(cols[0:own, 16 + o:17 + o], (own, 128))
    cols[group_rows:group_rows + 8, :] = jnp.broadcast_to(scale_of(RING)[:, 0:1], (8, 128))

    for s in range(2):
        h = (a + s) % HALVES
        comes = jnp.logical_or(jnp.logical_and(h == HALVES - 1, g < groups - 1),
                               jnp.logical_and(h != HALVES - 1, level != LEVELS - 1))

        @pl.when(comes)
        def _():
            remote(nrstage.at[0], nr.at[s], nr_send.at[0], nr_recv.at[s], g, (z + 1) % RING).wait_recv()

        factor = cols[pl.ds(pl.multiple_of((h + 1) * half, 8), 8), :][0:1, LEVELS - 1:LEVELS]
        nrn[s] = nr[s].astype(F32) * factor
    for s in range(2):
        own_loads[s].wait()

    last = lax.broadcasted_iota(jnp.int32, (CHUNK, 128), 0) == CHUNK - 1

    def work(i, _):
        k = chunks - 1 - i
        s, kk = k // per_half, k % per_half
        row = pl.multiple_of(((a + s) % HALVES) * half + kk * CHUNK, CHUNK)
        at = pl.multiple_of(k * CHUNK, CHUNK)
        level_copy(1, k).wait_recv()
        level_copy(2, k).wait_recv()

        @pl.when(kk == per_half - 1)
        def _():
            nxt[...] = nrn[s]

        tile = cols[pl.ds(row, CHUNK), :]
        scales = [jnp.broadcast_to(tile[:, l:l + 1], (CHUNK, 128)) for l in range(LEVELS)]
        ok = val[pl.ds(row, CHUNK), :]
        loss = jnp.zeros((CHUNK, 128), F32)
        for b in range(blocks):
            cs = slice(128 * b, 128 * b + 128)
            unit = [xbuf[l, pl.ds(at, CHUNK), cs].astype(F32) * scales[l] for l in range(LEVELS)]
            joined = unit[0] * gbuf[0:1, cs] + unit[1] * gbuf[1:2, cs] + unit[2] * gbuf[2:3, cs]
            mixbuf[pl.ds(at, CHUNK), cs] = joined.astype(BF16)
            target = jnp.where(last, nxt[b:b + 1, :], pltpu.roll(unit[2], CHUNK - 1, 0))
            nxt[b:b + 1, :] = unit[2][0:1, :]
            error = joined - target
            slope = jnp.clip(error, -1.0, 1.0)
            loss = loss + slope * (error - 0.5 * slope)
            slope = slope * ok
            for l in range(LEVELS):
                term = slope * unit[l]
                acc[l, :, cs] = acc[l, :, cs] + (term[0:8] + term[8:16])
        lq[s, pl.ds(pl.multiple_of(kk * CHUNK, CHUNK), CHUNK), :] = loss * ok
        return 0

    lax.fori_loop(0, chunks, work, 0)

    factor = 1.0 / (math.sqrt(total_rows) * LEVELS)
    part[...] = jnp.zeros(part.shape, F32)
    for l in range(LEVELS):
        for b in range(blocks):
            r = l * per_piece + b % per_piece
            part[b // per_piece, r:r + 1, :] = factor * jnp.sum(acc[l, :, 128 * b:128 * b + 128], axis=0, keepdims=True)

    def a_copy(j):
        return remote(part.at[(y + j) % ny], ra.at[y], ar_send.at[0, j], ar_recv.at[0, j], y_peer(j), z)

    for j in range(1, ny):
        a_copy(j).start()
    ra[y] = part[y]

    for s in range(2):
        lrow[s] = jnp.sum(lq[s].T, axis=0, keepdims=True)

    def mixed_copy(s, q):
        owner = 2 * ((a + s) % HALVES) + q
        return owner, remote(mixbuf.at[pl.ds(s * half + 32 * q, 48), :], obuf.at[quarter],
                             p2_send.at[2 * s + q], p2_recv.at[quarter], g, owner)

    def loss_copy(s, q):
        owner = 2 * ((a + s) % HALVES) + q
        return owner, remote(lrow.at[s], lbuf.at[quarter], ls_send.at[2 * s + q], ls_recv.at[quarter], g, owner)

    for s in range(2):
        for q in range(2):
            owner, copy = mixed_copy(s, q)
            _, small = loss_copy(s, q)

            @pl.when(owner != z)
            def _():
                copy.start()
                small.start()

            @pl.when(owner == z)
            def _():
                obuf[quarter] = mixbuf[s * half + 32 * q:s * half + 32 * q + 48, :]
                lbuf[quarter] = lrow[s]

    for j in range(1, ny):
        a_copy(j).wait_recv()
    total = ra[0]
    for j in range(1, ny):
        total = total + ra[j]
    sa[...] = total

    me = x * nk + kc

    def b_copy(j):
        return remote(sa, rb.at[me], ar_send.at[1, j], ar_recv.at[1, j], xk_peer(j), z)

    for j in range(1, nx * nk):
        b_copy(j).start()
    rb[me] = sa[...]
    for j in range(1, nx * nk):
        b_copy(j).wait_recv()
    total = rb[0]
    for j in range(1, nx * nk):
        total = total + rb[j]
    sb[...] = total

    def c_copy(j):
        return remote(sb, rc.at[level], ar_send.at[2, j], ar_recv.at[2, j], g, (z + QUARTERS * j) % RING)

    for j in range(1, LEVELS):
        c_copy(j).start()
    rc[level] = sb[...]
    for j in range(1, LEVELS):
        c_copy(j).wait_recv()
    gd[y, quarter] = rc[0] + rc[1] + rc[2]

    def d_copy(j):
        return remote(gd.at[y, quarter], gd.at[y, quarter], ar_send.at[3, j], ar_recv.at[3, j],
                      g, QUARTERS * level + (quarter + j) % QUARTERS)

    for j in range(1, QUARTERS):
        d_copy(j).start()
    for j in range(1, QUARTERS):
        d_copy(j).wait_recv()

    def e_copy(j):
        return remote(gd.at[y], gd.at[y], ar_send.at[4, j], ar_recv.at[4, j], y_peer(j), z)

    for j in range(1, ny):
        e_copy(j).start()

    mine, odd = z // 2, z % 2
    for i in range(QUARTERS):
        @pl.when(QUARTERS * handler_level(mine, i) + i != z)
        def _():
            remote(mixbuf.at[pl.ds(0, 48), :], obuf.at[i], p2_send.at[0], p2_recv.at[i], g, (z + 1) % RING).wait_recv()
            remote(lrow.at[0], lbuf.at[i], ls_send.at[0], ls_recv.at[i], g, (z + 1) % RING).wait_recv()

    total = lbuf[0] + lbuf[1] + lbuf[2] + lbuf[3]
    row_loss[...] = total * (1.0 / (QUARTERS * width))

    @pl.when(odd == 0)
    def _():
        for i in range(QUARTERS):
            mixed[:, i * width:(i + 1) * width] = obuf[i, 0:own, :]

    @pl.when(odd == 1)
    def _():
        for i in range(QUARTERS):
            for b in range(0, width, 256):
                rows = obuf[i, :, b:b + 256].astype(F32)
                mixed[:, i * width + b:i * width + b + 256] = rows[8:8 + own, :].astype(BF16)

    for j in range(1, ny):
        e_copy(j).wait_recv()
    for q in range(QUARTERS):
        for j in range(ny):
            for l in range(LEVELS):
                for i in range(per_piece):
                    at = q * width + (j * per_piece + i) * 128
                    grads[l:l + 1, at:at + 128] = gd[j, q, l * per_piece + i:l * per_piece + i + 1, :]

    for j in range(1, RING):
        m1_copy(j).wait_send()

    @pl.when(sends_back)
    def _():
        for i in range(4):
            edge_copy(i).wait_send()

    for h in range(HALVES):
        @pl.when(next_goes(h))
        def _():
            next_copy(h).wait_send()

    def level_sent(k, _):
        level_copy(1, k).wait_send()
        level_copy(2, k).wait_send()
        return 0

    lax.fori_loop(0, chunks, level_sent, 0)
    for s in range(2):
        for q in range(2):
            owner, copy = mixed_copy(s, q)
            _, small = loss_copy(s, q)

            @pl.when(owner != z)
            def _():
                copy.wait_send()
                small.wait_send()

    for j in range(1, ny):
        a_copy(j).wait_send()
        e_copy(j).wait_send()
    for j in range(1, nx * nk):
        b_copy(j).wait_send()
    for j in range(1, LEVELS):
        c_copy(j).wait_send()
    for j in range(1, QUARTERS):
        d_copy(j).wait_send()


def solution(mesh):
    groups = mesh.shape["dp"]
    nk = 2
    ny = 8 if groups == 64 else groups // nk
    nx = groups // (nk * ny)

    def shards(features, segment, gains):
        rows, width = features.shape
        own = rows // RING
        sizes = (groups, nx, ny, nk, own, width, rows * groups)
        half = 2 * own
        lanes = -(-rows // 128) * 128
        seg = jnp.pad(segment.astype(F32).reshape(1, own), ((0, 0), (0, 128 - own)))
        vmem = pl.BlockSpec(memory_space=pltpu.VMEM)
        hbm = pl.BlockSpec(memory_space=pl.ANY)
        dma = pltpu.SemaphoreType.DMA
        chunks = 2 * half // CHUNK
        mixed, grads, row_loss = pl.pallas_call(
            functools.partial(kernel, sizes),
            out_shape=(
                jax.ShapeDtypeStruct((own, QUARTERS * width), BF16),
                jax.ShapeDtypeStruct((LEVELS, QUARTERS * width), F32),
                jax.ShapeDtypeStruct((1, 128), F32),
            ),
            in_specs=[hbm, vmem, hbm],
            out_specs=(vmem, vmem, vmem),
            scratch_shapes=[
                pltpu.VMEM((rows, width), BF16),
                pltpu.VMEM((LEVELS, 2 * half, width), BF16),
                pltpu.VMEM((LEVELS, width), F32),
                pltpu.VMEM((2 * half, width), BF16),
                pltpu.VMEM((QUARTERS, 48, width), BF16),
                pltpu.VMEM((RING + 5, 1, lanes + 128), F32),
                pltpu.VMEM((2, 16, 128), BF16),
                pltpu.VMEM((16, 128), F32),
                pltpu.VMEM((HALVES, 16, 128), BF16),
                pltpu.VMEM((2, 16, 128), F32),
                pltpu.VMEM((16, 128), F32),
                pltpu.VMEM((lanes, 128), F32),
                pltpu.VMEM((16, 128), F32),
                pltpu.VMEM((128, lanes), F32),
                pltpu.VMEM((lanes, 128), F32),
                pltpu.VMEM((rows, 128), F32),
                pltpu.VMEM((LEVELS, 8, width), F32),
                pltpu.VMEM((2, 128, 128), F32),
                pltpu.VMEM((2, 1, 128), F32),
                pltpu.VMEM((QUARTERS, 1, 128), F32),
                pltpu.VMEM((ny, 8, 128), F32),
                pltpu.VMEM((ny, 8, 128), F32),
                pltpu.VMEM((8, 128), F32),
                pltpu.VMEM((nx * nk, 8, 128), F32),
                pltpu.VMEM((8, 128), F32),
                pltpu.VMEM((LEVELS, 8, 128), F32),
                pltpu.VMEM((ny, QUARTERS, 8, 128), F32),
                dma((HALVES + 3,)),
                dma((2, chunks)), dma((2, chunks)),
                dma((RING - 1,)), dma((RING - 1,)),
                dma((4,)), dma((5,)),
                dma((HALVES,)), dma((2,)),
                dma((4,)), dma((QUARTERS,)),
                dma((4,)), dma((QUARTERS,)),
                dma((5, 8)), dma((5, 8)),
            ],
            compiler_params=pltpu.CompilerParams(
                collective_id=0, has_side_effects=True, vmem_limit_bytes=32 * 1024 * 1024),
        )(features, seg, gains)
        start = (lax.axis_index("mp") % 2) * own
        row_loss = lax.dynamic_slice_in_dim(row_loss.reshape(128), start, own, 0)
        return mixed, grads, row_loss

    return jax.shard_map(
        shards,
        mesh=mesh,
        in_specs=(P("dp", "mp"), P(("dp", "mp")), P()),
        out_specs=(P(("dp", "mp"), None), P(), P(("dp", "mp"))),
        check_vma=False,
    )
```

time: 603 us -> 110 us (0.18)
  waiting for transfers between devices: 465 us -> 0 us
  Pallas kernels: 0 us -> 103 us
  starting transfers between devices: 74 us -> 0 us
  local copies, waits for them, and re-layouts: 29.9 us -> 4.53 us
  other arithmetic: 17.3 us -> 0.66 us
  between operations: 14.9 us -> 0.67 us
    psum x1 -> x0, waiting for transfers between devices: 451 us -> none  [shards(): grad_gains = lax.psum(local_grad, ('dp', 'mp'))]
    pallas_call x0 -> x1, Pallas kernels: none -> 103 us  [shards(): pl.pallas_call(functools.partial(kernel, sizes), out_shape=(jax.ShapeDtyp...]
    ppermute x2 -> x0, starting transfers between devices: 58.3 us -> none  [passed_along(): return lax.ppermute(shard, axis, pairs)]
    reduce_sum x6 -> x0, other arithmetic: 16.1 us -> none  [the longest x1 7.39 us: shards(): joined = jnp.sum(unit * gains[None], axis=1) / 3.0]
    all_to_all x1 -> x0, starting transfers between devices: 15.7 us -> none  [shards(): lax.all_to_all(features, 'mp', split_axis=0, concat_axis=1, tiled=True)]
    convert_element_type x2 -> x0, local copies, waits for them, and re-layouts: 12.7 us -> none  [shards(): x = rows.astype(jnp.float32).reshape(count, 3, width)]
    mul x4 -> x0, local copies, waits for them, and re-layouts: 11.7 us -> none  [the longest x2 11.7 us: shards(): slope[:, None, :] * unit]
    ppermute x2 -> x0, waiting for transfers between devices: 9.25 us -> none  [passed_along(): return lax.ppermute(shard, axis, pairs)]
  transfers between devices with their start and end apart: 4 -> 0, of which waited for: 3 -> 0; matrix products, arithmetic and copies ran while one was open for 4% -> 0% of each run, Pallas kernels for 0% -> 0%
where the time goes in v1:
time: 110 us; the launch traced here: 109 us
  Pallas kernels  103 us (94%)
  local copies, waits for them, and re-layouts  4.53 us (4%)
    pallas_call x1, Pallas kernels, shards(): pl.pallas_call(functools.partial(kernel, sizes), out_shape=(jax.ShapeDtyp...  103 us
    unnamed x6, local copies, waits for them, and re-layouts  3.94 us

profile of v1, /device:TPU:1, one launch (start us, length us, event | category | flops | bytes accessed | tf_op | source)
XLA Modules:
  0.0 108.9 jit_solution(17902462950780287826)
XLA Ops:
  0.7 0.7 convert_bitcast_fusion
  1.3 0.0 copy-start
  1.3 1.5 %copy-done = bf16[480,2048]{1,0:T(8,128)(2,1)S(1)} copy-done((bf16[480,2048]{1,0:T(8,128)(2,1)S(1)}, bf16[480,2048]{1,0:T(8,128)(2,1)}, u32[]{:S(2)}) %copy-start) | copy-done | bytes 1966104
  2.9 0.0 copy-start.1
  2.9 0.9 copy-done.1
  3.8 103.0 %shard_map.58 = (bf16[40,8192]{1,0:T(8,128)(2,1)S(1)}, f32[3,8192]{1,0:T(4,128)S(1)}, f32[1,128]{1,0:T(1,128)S(1)}) custom-call(bf16[480,2048]{1,0:T(8,128)(2,1)S(1)} %copy-done, f32[1,128]{1,0:T(1,128)S(1)} %pad.4.seg, f32[3,8192]{1,0:T(4,128)S(1)} %copy-done.1), custom_call_target="tpu_custom_call" | custom-call | tf_op jit(solution)/shard_map/pallas_call | solution.py:453
  106.8 0.6 dynamic-slice_bitcast_fusion
  107.4 0.8 copy.8
  108.2 0.7 copy.9
  (1 shorter events, 0.0 us)
Async XLA Ops:
  1.3 1.5 %copy-start = (bf16[480,2048]{1,0:T(8,128)(2,1)S(1)}, bf16[480,2048]{1,0:T(8,128)(2,1)}, u32[]{:S(2)}) copy-start(bf16[480,2048]{1,0:T(8,128)(2,1)} %feat.1) | copy-start | bytes 5898244
  2.9 0.9 copy-start.1

commit v2 on v1

--- a/solution.py
+++ b/solution.py
@@ -26,37 +26,35 @@
     return (((half + HALVES + 1 - (quarter + 1) // 2) % HALVES)) // 2
 
 
-def kernel(sizes, feat, seg, gains, mixed, grads, row_loss, fbuf, xbuf, gbuf, mixbuf, obuf, m1, nr, nrs, nrstage, nrn, nxt,
-           sq, segs, scp, cols, val, acc, lq, lrow, lbuf, part, ra, sa, rb, sb, rc, gd,
+def kernel(sizes, feat, seg, gains, mixed, grads, row_loss, fbuf, xbuf, gbuf, segbuf, mixbuf, obuf, m1, nr, nrs, nrstage, nrn, nxt,
+           sq, segs, scp, cols, val, acc, lq, lrow, lbuf, part, kb, sa, rb, rc, gf,
            local_sem, p1_send, p1_recv, m1_send, m1_recv, mx_send, mx_recv, nr_send, nr_recv, p2_send, p2_recv,
-           ls_send, ls_recv, ar_send, ar_recv):
+           ls_send, ls_recv, k_sem, xy_sem, z_sem, y_send, y_recv, f_send, f_recv):
     groups, nx, ny, nk, own, width, total_rows = sizes
     half = 2 * own
     group_rows = HALVES * half
     per_half = half // CHUNK
     chunks = 2 * per_half
     blocks = width // 128
-    per_piece = blocks // ny
+    per_piece = blocks // (ny * nk)
     lanes = m1.shape[2] - 128
 
     g, z = lax.axis_index("dp"), lax.axis_index("mp")
-    level, quarter = z // QUARTERS, z % QUARTERS
+    level, quarter = lax.div(z, QUARTERS), lax.rem(z, QUARTERS)
     a = first_half(level, quarter)
-    kc = g % nk
-    y = (g // nk) % ny
-    x = g // (nk * ny)
+    kc = lax.rem(g, nk)
+    y = lax.rem(lax.div(g, nk), ny)
+    x = lax.div(g, nk * ny)
+    xs = [lax.rem(x + i, nx) * (ny * nk) + kc for i in range(nx)]
+    ys = [lax.rem(y + i, ny) for i in range(ny)]
+    zs = [lax.rem(z + i, RING) for i in range(RING)]
+    plane = [(dx, dy) for dx in range(nx) for dy in range(ny)][1:]
+    other = g + 1 - 2 * kc
 
     def remote(src, dst, send, recv, gd_, zd_):
         return pltpu.make_async_remote_copy(
             src_ref=src, dst_ref=dst, send_sem=send, recv_sem=recv,
             device_id=(gd_, zd_), device_id_type=pl.DeviceIdType.MESH)
-
-    def y_peer(j):
-        return (x * ny + (y + j) % ny) * nk + kc
-
-    def xk_peer(j):
-        n = (x * nk + kc + j) % (nx * nk)
-        return ((n // nk) * ny + y) * nk + n % nk
 
     loads = []
     for h in range(HALVES):
@@ -66,6 +64,8 @@
     gain_load = pltpu.make_async_copy(
         gains.at[:, pl.ds(pl.multiple_of(quarter * width, width), width)], gbuf, local_sem.at[HALVES])
     gain_load.start()
+    seg_load = pltpu.make_async_copy(seg, segbuf, local_sem.at[HALVES + 3])
+    seg_load.start()
     own_loads = []
     for s in range(2):
         row = pl.multiple_of(((a + s) % HALVES) * half, half)
@@ -86,12 +86,11 @@
     def greet(gd_, zd_):
         pl.semaphore_signal(barrier, inc=1, device_id=(gd_, zd_), device_id_type=pl.DeviceIdType.MESH)
 
-    for j in range(1, RING):
-        greet(g, (z + j) % RING)
-    for j in range(1, ny):
-        greet(y_peer(j), z)
-    for j in range(1, nx * nk):
-        greet(xk_peer(j), z)
+    for j in (QUARTERS, 2 * QUARTERS, 1, 11, 2, 10, 3, 9, 5, 7, 6):
+        greet(g, zs[j])
+    greet(other, z)
+    for dx, dy in plane:
+        greet(xs[dx] + ys[dy] * nk, z)
 
     @pl.when(sends_back)
     def _():
@@ -118,7 +117,9 @@
 
         lax.fori_loop(0, per_half, squares, 0)
     m1[z, :, 0:lanes] = jnp.sum(sq[...].T, axis=0, keepdims=True)
-    m1[z, :, lanes:lanes + 128] = seg[...]
+    seg_load.wait()
+    m1[z, :, lanes:lanes + 128] = jnp.zeros((1, 128), F32)
+    m1[z, :, lanes:lanes + own] = segbuf[...].astype(F32)
 
     @pl.when(level == LEVELS - 1)
     def _():
@@ -130,11 +131,10 @@
             nrstage[h] = nrs[...].astype(BF16)
 
     pl.semaphore_wait(
-        barrier,
-        (RING - 1) + (ny - 1) + (nx * nk - 1) + jnp.where(sends_back, 4, 0) + jnp.where(hears_next, 5, 0))
+        barrier, RING - 1 + nk - 1 + len(plane) + jnp.where(sends_back, 4, 0) + jnp.where(hears_next, 5, 0))
 
     def m1_copy(j):
-        return remote(m1.at[z], m1.at[z], m1_send.at[j - 1], m1_recv.at[j - 1], g, (z + j) % RING)
+        return remote(m1.at[z], m1.at[z], m1_send.at[j - 1], m1_recv.at[j - 1], g, zs[j])
 
     for j in range(1, RING):
         m1_copy(j).start()
@@ -276,20 +276,24 @@
 
     factor = 1.0 / (math.sqrt(total_rows) * LEVELS)
     part[...] = jnp.zeros(part.shape, F32)
-    for l in range(LEVELS):
-        for b in range(blocks):
-            r = l * per_piece + b % per_piece
-            part[b // per_piece, r:r + 1, :] = factor * jnp.sum(acc[l, :, 128 * b:128 * b + 128], axis=0, keepdims=True)
-
-    def a_copy(j):
-        return remote(part.at[(y + j) % ny], ra.at[y], ar_send.at[0, j], ar_recv.at[0, j], y_peer(j), z)
-
-    for j in range(1, ny):
-        a_copy(j).start()
-    ra[y] = part[y]
+    for b in range(blocks):
+        for l in range(LEVELS):
+            part[b % nk, b // nk, l:l + 1, :] = factor * jnp.sum(acc[l, :, 128 * b:128 * b + 128], axis=0, keepdims=True)
+    k_copy = remote(part.at[1 - kc], kb, k_sem.at[0], k_sem.at[1], other, z)
+    k_copy.start()
 
     for s in range(2):
         lrow[s] = jnp.sum(lq[s].T, axis=0, keepdims=True)
+
+    k_copy.wait_recv()
+    sa[...] = part[kc] + kb[...]
+
+    def xy_copy(n):
+        dx, dy = plane[n]
+        return remote(sa.at[ys[dy]], rb.at[n], xy_sem.at[0], xy_sem.at[1], xs[dx] + ys[dy] * nk, z)
+
+    for n in range(len(plane)):
+        xy_copy(n).start()
 
     def mixed_copy(s, q):
         owner = 2 * ((a + s) % HALVES) + q
@@ -315,52 +319,51 @@
                 obuf[quarter] = mixbuf[s * half + 32 * q:s * half + 32 * q + 48, :]
                 lbuf[quarter] = lrow[s]
 
+    for j in range(1, RING):
+        m1_copy(j).wait_send()
+
+    @pl.when(sends_back)
+    def _():
+        for i in range(4):
+            edge_copy(i).wait_send()
+
+    for h in range(HALVES):
+        @pl.when(next_goes(h))
+        def _():
+            next_copy(h).wait_send()
+
+    def level_sent(k, _):
+        level_copy(1, k).wait_send()
+        level_copy(2, k).wait_send()
+        return 0
+
+    lax.fori_loop(0, chunks, level_sent, 0)
+    pltpu.make_async_copy(rb, rb, xy_sem.at[1]).wait()
+    total = sa[y]
+    for n in range(len(plane)):
+        total = total + rb[n]
+    rc[0] = total
+
+    def z_copy(j):
+        return remote(rc.at[0], rc.at[j], z_sem.at[0], z_sem.at[1], g, zs[j])
+
+    for j in range(1, RING):
+        z_copy(j).start()
+    landed = rc.at[pl.ds(1, RING - 1)]
+    pltpu.make_async_copy(landed, landed, z_sem.at[1]).wait()
+    for j in range(QUARTERS):
+        gf[kc, y, lax.rem(quarter + QUARTERS - j, QUARTERS)] = rc[j] + rc[j + QUARTERS] + rc[j + 2 * QUARTERS]
+
+    def y_copy(j):
+        return remote(gf.at[kc, y], gf.at[kc, y], y_send.at[j], y_recv.at[j], xs[0] + ys[j] * nk, z)
+
+    def f_copy(j):
+        at = lax.rem(y + ny - j, ny)
+        return remote(gf.at[kc, at], gf.at[kc, at], f_send.at[j], f_recv.at[j], other, z)
+
     for j in range(1, ny):
-        a_copy(j).wait_recv()
-    total = ra[0]
-    for j in range(1, ny):
-        total = total + ra[j]
-    sa[...] = total
-
-    me = x * nk + kc
-
-    def b_copy(j):
-        return remote(sa, rb.at[me], ar_send.at[1, j], ar_recv.at[1, j], xk_peer(j), z)
-
-    for j in range(1, nx * nk):
-        b_copy(j).start()
-    rb[me] = sa[...]
-    for j in range(1, nx * nk):
-        b_copy(j).wait_recv()
-    total = rb[0]
-    for j in range(1, nx * nk):
-        total = total + rb[j]
-    sb[...] = total
-
-    def c_copy(j):
-        return remote(sb, rc.at[level], ar_send.at[2, j], ar_recv.at[2, j], g, (z + QUARTERS * j) % RING)
-
-    for j in range(1, LEVELS):
-        c_copy(j).start()
-    rc[level] = sb[...]
-    for j in range(1, LEVELS):
-        c_copy(j).wait_recv()
-    gd[y, quarter] = rc[0] + rc[1] + rc[2]
-
-    def d_copy(j):
-        return remote(gd.at[y, quarter], gd.at[y, quarter], ar_send.at[3, j], ar_recv.at[3, j],
-                      g, QUARTERS * level + (quarter + j) % QUARTERS)
-
-    for j in range(1, QUARTERS):
-        d_copy(j).start()
-    for j in range(1, QUARTERS):
-        d_copy(j).wait_recv()
-
-    def e_copy(j):
-        return remote(gd.at[y], gd.at[y], ar_send.at[4, j], ar_recv.at[4, j], y_peer(j), z)
-
-    for j in range(1, ny):
-        e_copy(j).start()
+        y_copy(j).start()
+    f_copy(0).start()
 
     mine, odd = z // 2, z % 2
     for i in range(QUARTERS):
@@ -370,7 +373,8 @@
             remote(lrow.at[0], lbuf.at[i], ls_send.at[0], ls_recv.at[i], g, (z + 1) % RING).wait_recv()
 
     total = lbuf[0] + lbuf[1] + lbuf[2] + lbuf[3]
-    row_loss[...] = total * (1.0 / (QUARTERS * width))
+    total = total * (1.0 / (QUARTERS * width))
+    row_loss[...] = jnp.where(odd == 0, total[:, 0:own], total[:, own:2 * own])
 
     @pl.when(odd == 0)
     def _():
@@ -384,34 +388,16 @@
                 rows = obuf[i, :, b:b + 256].astype(F32)
                 mixed[:, i * width + b:i * width + b + 256] = rows[8:8 + own, :].astype(BF16)
 
-    for j in range(1, ny):
-        e_copy(j).wait_recv()
+    for j in sorted(range(1, ny), key=lambda j: min(j, ny - j)):
+        y_copy(j).wait_recv()
+        f_copy(j).start()
+    for j in range(ny):
+        f_copy(j).wait_recv()
     for q in range(QUARTERS):
-        for j in range(ny):
-            for l in range(LEVELS):
-                for i in range(per_piece):
-                    at = q * width + (j * per_piece + i) * 128
-                    grads[l:l + 1, at:at + 128] = gd[j, q, l * per_piece + i:l * per_piece + i + 1, :]
-
-    for j in range(1, RING):
-        m1_copy(j).wait_send()
-
-    @pl.when(sends_back)
-    def _():
-        for i in range(4):
-            edge_copy(i).wait_send()
-
-    for h in range(HALVES):
-        @pl.when(next_goes(h))
-        def _():
-            next_copy(h).wait_send()
-
-    def level_sent(k, _):
-        level_copy(1, k).wait_send()
-        level_copy(2, k).wait_send()
-        return 0
-
-    lax.fori_loop(0, chunks, level_sent, 0)
+        for b in range(blocks):
+            at = q * width + b * 128
+            grads[:, at:at + 128] = gf[b % nk, b // nk, q, 0:LEVELS, :]
+
     for s in range(2):
         for q in range(2):
             owner, copy = mixed_copy(s, q)
@@ -422,15 +408,24 @@
                 copy.wait_send()
                 small.wait_send()
 
+    k_copy.wait_send()
+    pltpu.make_async_copy(rb, rb, xy_sem.at[0]).wait()
+    pltpu.make_async_copy(landed, landed, z_sem.at[0]).wait()
     for j in range(1, ny):
-        a_copy(j).wait_send()
-        e_copy(j).wait_send()
-    for j in range(1, nx * nk):
-        b_copy(j).wait_send()
-    for j in range(1, LEVELS):
-        c_copy(j).wait_send()
-    for j in range(1, QUARTERS):
-        d_copy(j).wait_send()
+        y_copy(j).wait_send()
+    for j in range(ny):
+        f_copy(j).wait_send()
+
+
+def hand_over(mixed, grads, row_loss, mixed_out, grads_out, loss_out, sem):
+    copies = [
+        pltpu.make_async_copy(src, dst, sem.at[i])
+        for i, (src, dst) in enumerate(((mixed, mixed_out), (grads, grads_out), (row_loss, loss_out)))
+    ]
+    for copy in copies:
+        copy.start()
+    for copy in copies:
+        copy.wait()
 
 
 def solution(mesh):
@@ -445,9 +440,8 @@
         sizes = (groups, nx, ny, nk, own, width, rows * groups)
         half = 2 * own
         lanes = -(-rows // 128) * 128
-        seg = jnp.pad(segment.astype(F32).reshape(1, own), ((0, 0), (0, 128 - own)))
         vmem = pl.BlockSpec(memory_space=pltpu.VMEM)
-        hbm = pl.BlockSpec(memory_space=pl.ANY)
+        hbm = pl.BlockSpec(memory_space=pltpu.HBM)
         dma = pltpu.SemaphoreType.DMA
         chunks = 2 * half // CHUNK
         mixed, grads, row_loss = pl.pallas_call(
@@ -455,14 +449,15 @@
             out_shape=(
                 jax.ShapeDtypeStruct((own, QUARTERS * width), BF16),
                 jax.ShapeDtypeStruct((LEVELS, QUARTERS * width), F32),
-                jax.ShapeDtypeStruct((1, 128), F32),
+                jax.ShapeDtypeStruct((1, own), F32),
             ),
-            in_specs=[hbm, vmem, hbm],
+            in_specs=[hbm, hbm, hbm],
             out_specs=(vmem, vmem, vmem),
             scratch_shapes=[
                 pltpu.VMEM((rows, width), BF16),
                 pltpu.VMEM((LEVELS, 2 * half, width), BF16),
                 pltpu.VMEM((LEVELS, width), F32),
+                pltpu.VMEM((1, own), jnp.int32),
                 pltpu.VMEM((2 * half, width), BF16),
                 pltpu.VMEM((QUARTERS, 48, width), BF16),
                 pltpu.VMEM((RING + 5, 1, lanes + 128), F32),
@@ -480,28 +475,33 @@
                 pltpu.VMEM((2, 128, 128), F32),
                 pltpu.VMEM((2, 1, 128), F32),
                 pltpu.VMEM((QUARTERS, 1, 128), F32),
-                pltpu.VMEM((ny, 8, 128), F32),
-                pltpu.VMEM((ny, 8, 128), F32),
-                pltpu.VMEM((8, 128), F32),
-                pltpu.VMEM((nx * nk, 8, 128), F32),
-                pltpu.VMEM((8, 128), F32),
-                pltpu.VMEM((LEVELS, 8, 128), F32),
-                pltpu.VMEM((ny, QUARTERS, 8, 128), F32),
-                dma((HALVES + 3,)),
+                pltpu.VMEM((nk, ny, 4, 128), F32),
+                pltpu.VMEM((ny, 4, 128), F32),
+                pltpu.VMEM((ny, 4, 128), F32),
+                pltpu.VMEM((nx * ny - 1, 4, 128), F32),
+                pltpu.VMEM((RING, 4, 128), F32),
+                pltpu.VMEM((nk, ny, QUARTERS, 4, 128), F32),
+                dma((HALVES + 4,)),
                 dma((2, chunks)), dma((2, chunks)),
                 dma((RING - 1,)), dma((RING - 1,)),
                 dma((4,)), dma((5,)),
                 dma((HALVES,)), dma((2,)),
                 dma((4,)), dma((QUARTERS,)),
                 dma((4,)), dma((QUARTERS,)),
-                dma((5, 8)), dma((5, 8)),
+                dma((2,)), dma((2,)), dma((2,)), dma((ny,)), dma((ny,)), dma((ny,)), dma((ny,)),
             ],
             compiler_params=pltpu.CompilerParams(
                 collective_id=0, has_side_effects=True, vmem_limit_bytes=32 * 1024 * 1024),
-        )(features, seg, gains)
-        start = (lax.axis_index("mp") % 2) * own
-        row_loss = lax.dynamic_slice_in_dim(row_loss.reshape(128), start, own, 0)
-        return mixed, grads, row_loss
+        )(*(pltpu.with_memory_space_constraint(v, pltpu.HBM) for v in (features, segment.reshape(1, own), gains)))
+        mixed, grads, row_loss = pl.pallas_call(
+            hand_over,
+            out_shape=tuple(jax.ShapeDtypeStruct(v.shape, v.dtype) for v in (mixed, grads, row_loss)),
+            in_specs=[vmem] * 3,
+            out_specs=(hbm,) * 3,
+            scratch_shapes=[dma((3,))],
+            compiler_params=pltpu.CompilerParams(vmem_limit_bytes=4 * 1024 * 1024),
+        )(mixed, grads, row_loss)
+        return mixed, grads, row_loss.reshape(own)
 
     return jax.shard_map(
         shards,

time: 110 us -> 105 us (0.955)
  local copies, waits for them, and re-layouts: 4.53 us -> 0 us
    unnamed x6 -> x0, local copies, waits for them, and re-layouts: 3.94 us -> none
where the time goes in v2:
time: 105 us
  Pallas kernels  104 us (99%)
    pallas_call x1, Pallas kernels, shards(): pl.pallas_call(functools.partial(kernel, sizes), out_shape=(jax.ShapeDtyp...  103 us

profile of v2, /device:TPU:1, one launch (start us, length us, event | category | flops | bytes accessed | tf_op | source)
XLA Modules:
  0.0 104.8 jit_solution(1624908939636797126)
XLA Ops:
  0.6 103.3 %shard_map.58 = (bf16[40,8192]{1,0:T(8,128)(2,1)S(1)}, f32[3,8192]{1,0:T(4,128)S(1)}, f32[1,40]{1,0:T(1,128)S(1)}) custom-call(bf16[480,2048]{1,0:T(8,128)(2,1)} %feat.1, s32[1,40]{1,0:T(1,128)} %bitcast.2, f32[3,8192]{1,0:T(4,128)} %gains.1), custom_call_target="tpu_custom_call" | custom-call | tf_op jit(solution)/shard_map/pallas_call | solution.py:447
  103.9 0.9 shard_map.59

commit v3 on v2

--- a/solution.py
+++ b/solution.py
@@ -49,12 +49,42 @@
     ys = [lax.rem(y + i, ny) for i in range(ny)]
     zs = [lax.rem(z + i, RING) for i in range(RING)]
     plane = [(dx, dy) for dx in range(nx) for dy in range(ny)][1:]
+    plane.sort(key=lambda p: -min(p[0], nx - p[0]) - min(p[1], ny - p[1]))
     other = g + 1 - 2 * kc
 
     def remote(src, dst, send, recv, gd_, zd_):
         return pltpu.make_async_remote_copy(
             src_ref=src, dst_ref=dst, send_sem=send, recv_sem=recv,
             device_id=(gd_, zd_), device_id_type=pl.DeviceIdType.MESH)
+
+    m1[pl.ds(RING, 5), :, 0:lanes] = jnp.zeros((5, 1, lanes), F32)
+    m1[pl.ds(RING, 5), :, lanes:lanes + 128] = jnp.full((5, 1, 128), -1.0, F32)
+    nr[...] = jnp.zeros(nr.shape, BF16)
+
+    sends_back = jnp.logical_and(jnp.logical_or(z == 0, z >= 2 * QUARTERS), g > 0)
+    hears_next = jnp.logical_and(jnp.logical_or(z == 0, z > 2 * QUARTERS), g < groups - 1)
+    edge_in = (0, 9, 10, 11)
+    edge_out = (8, 9, 10, 11, 0)
+    barrier = pltpu.get_barrier_semaphore()
+
+    def greet(gd_, zd_):
+        pl.semaphore_signal(barrier, inc=1, device_id=(gd_, zd_), device_id_type=pl.DeviceIdType.MESH)
+
+    for j in (QUARTERS, 2 * QUARTERS, 1, 11, 2, 10, 3, 9, 5, 7, 6):
+        greet(g, zs[j])
+    @pl.when(sends_back)
+    def _():
+        for zd in edge_in:
+            greet(g - 1, zd)
+
+    @pl.when(hears_next)
+    def _():
+        for zd in edge_out:
+            greet(g + 1, zd)
+
+    greet(other, z)
+    for dx, dy in plane:
+        greet(xs[dx] + ys[dy] * nk, z)
 
     loads = []
     for h in range(HALVES):
@@ -72,35 +102,6 @@
         own_loads.append(pltpu.make_async_copy(
             feat.at[pl.ds(row, half), :], xbuf.at[level, pl.ds(s * half, half), :], local_sem.at[HALVES + 1 + s]))
         own_loads[-1].start()
-
-    m1[pl.ds(RING, 5), :, 0:lanes] = jnp.zeros((5, 1, lanes), F32)
-    m1[pl.ds(RING, 5), :, lanes:lanes + 128] = jnp.full((5, 1, 128), -1.0, F32)
-    nr[...] = jnp.zeros(nr.shape, BF16)
-
-    sends_back = jnp.logical_and(jnp.logical_or(z == 0, z >= 2 * QUARTERS), g > 0)
-    hears_next = jnp.logical_and(jnp.logical_or(z == 0, z > 2 * QUARTERS), g < groups - 1)
-    edge_in = (0, 9, 10, 11)
-    edge_out = (8, 9, 10, 11, 0)
-    barrier = pltpu.get_barrier_semaphore()
-
-    def greet(gd_, zd_):
-        pl.semaphore_signal(barrier, inc=1, device_id=(gd_, zd_), device_id_type=pl.DeviceIdType.MESH)
-
-    for j in (QUARTERS, 2 * QUARTERS, 1, 11, 2, 10, 3, 9, 5, 7, 6):
-        greet(g, zs[j])
-    greet(other, z)
-    for dx, dy in plane:
-        greet(xs[dx] + ys[dy] * nk, z)
-
-    @pl.when(sends_back)
-    def _():
-        for zd in edge_in:
-            greet(g - 1, zd)
-
-    @pl.when(hears_next)
-    def _():
-        for zd in edge_out:
-            greet(g + 1, zd)
 
     sq[pl.ds(group_rows, sq.shape[0] - group_rows), :] = jnp.zeros((sq.shape[0] - group_rows, 128), F32)
     for h in range(HALVES):
@@ -295,30 +296,6 @@
     for n in range(len(plane)):
         xy_copy(n).start()
 
-    def mixed_copy(s, q):
-        owner = 2 * ((a + s) % HALVES) + q
-        return owner, remote(mixbuf.at[pl.ds(s * half + 32 * q, 48), :], obuf.at[quarter],
-                             p2_send.at[2 * s + q], p2_recv.at[quarter], g, owner)
-
-    def loss_copy(s, q):
-        owner = 2 * ((a + s) % HALVES) + q
-        return owner, remote(lrow.at[s], lbuf.at[quarter], ls_send.at[2 * s + q], ls_recv.at[quarter], g, owner)
-
-    for s in range(2):
-        for q in range(2):
-            owner, copy = mixed_copy(s, q)
-            _, small = loss_copy(s, q)
-
-            @pl.when(owner != z)
-            def _():
-                copy.start()
-                small.start()
-
-            @pl.when(owner == z)
-            def _():
-                obuf[quarter] = mixbuf[s * half + 32 * q:s * half + 32 * q + 48, :]
-                lbuf[quarter] = lrow[s]
-
     for j in range(1, RING):
         m1_copy(j).wait_send()
 
@@ -349,6 +326,31 @@
 
     for j in range(1, RING):
         z_copy(j).start()
+
+    def mixed_copy(s, q):
+        owner = 2 * ((a + s) % HALVES) + q
+        return owner, remote(mixbuf.at[pl.ds(s * half + 32 * q, 48), :], obuf.at[quarter],
+                             p2_send.at[2 * s + q], p2_recv.at[quarter], g, owner)
+
+    def loss_copy(s, q):
+        owner = 2 * ((a + s) % HALVES) + q
+        return owner, remote(lrow.at[s], lbuf.at[quarter], ls_send.at[2 * s + q], ls_recv.at[quarter], g, owner)
+
+    for s in range(2):
+        for q in range(2):
+            owner, copy = mixed_copy(s, q)
+            _, small = loss_copy(s, q)
+
+            @pl.when(owner != z)
+            def _():
+                copy.start()
+                small.start()
+
+            @pl.when(owner == z)
+            def _():
+                obuf[quarter] = mixbuf[s * half + 32 * q:s * half + 32 * q + 48, :]
+                lbuf[quarter] = lrow[s]
+
     landed = rc.at[pl.ds(1, RING - 1)]
     pltpu.make_async_copy(landed, landed, z_sem.at[1]).wait()
     for j in range(QUARTERS):

time: 105 us -> 104 us (level)
    pallas_call x1, Pallas kernels: 103 us -> 102 us  [shards(): pl.pallas_call(functools.partial(kernel, sizes), out_shape=(jax.ShapeDtyp...]
where the time goes in v3:
time: 104 us
  Pallas kernels  103 us (99%)
    pallas_call x1, Pallas kernels, shards(): pl.pallas_call(functools.partial(kernel, sizes), out_shape=(jax.ShapeDtyp...  102 us

profile of v3, /device:TPU:1, one launch (start us, length us, event | category | flops | bytes accessed | tf_op | source)
XLA Modules:
  0.0 103.7 jit_solution(5352367779976823109)
XLA Ops:
  0.6 102.1 %shard_map.58 = (bf16[40,8192]{1,0:T(8,128)(2,1)S(1)}, f32[3,8192]{1,0:T(4,128)S(1)}, f32[1,40]{1,0:T(1,128)S(1)}) custom-call(bf16[480,2048]{1,0:T(8,128)(2,1)} %feat.1, s32[1,40]{1,0:T(1,128)} %bitcast.2, f32[3,8192]{1,0:T(4,128)} %gains.1), custom_call_target="tpu_custom_call" | custom-call | tf_op jit(solution)/shard_map/pallas_call | solution.py:449
  102.8 0.9 shard_map.59
